TPU v7x, 256 devices: a whole 4x4x8 slice. The times are simulated.
256 devices in a mesh: dp: 32 (over x, y, core), tensor: 8 (over z).
Axes of the slice: x: 4, y: 4, z: 8, core: 2. Of those that a mesh axis runs over, the one named last changes fastest.
Arguments:
- momentum: float32 [32, 5120, 1024], P('dp', None, 'tensor'), may hold values from -6 to 6
- activations: bfloat16 [32768, 5120], P(('dp', 'tensor')), may hold values from -6 to 6
- out_grads: bfloat16 [32768, 1024], P('dp', 'tensor'), may hold values from -0.29882812 to 0.29882812
- positions: int32 [32, 16, 4, 5120], P('dp', 'tensor'), may hold values from 0 to 63, as said below
Outputs:
- new_momentum: float32 [32, 5120, 1024], P('dp', None, 'tensor')
- update: bfloat16 [5120, 1024], P(None, 'tensor')
Inputs may be any that keep to these rules, and one draw needn't show every extreme that they name: The 4 positions of one block of one row of one replica are all different.
All inputs are finite; a program needn't handle non-finite values.
Results may differ from a plain program's by a relative error of at most 0.00075.
Values may be sent and summed in bfloat16 or wider, within the bound.
A program may use at most 128 MiB of HBM per device.

v0:
```python
import jax
import jax.numpy as jnp
from jax import lax
from jax.sharding import PartitionSpec as P


def sent_to_all(value, axis):
    copies = jnp.broadcast_to(value, (lax.axis_size(axis), *value.shape))
    return lax.all_to_all(copies, axis, split_axis=0, concat_axis=0, tiled=True)


def over_copies(value, axis):
    everything = sent_to_all(value, axis)
    return jnp.sum(everything, axis=0)


def dct_table():
    freq = jnp.arange(64, dtype=jnp.float32)[:, None]
    place = jnp.arange(64, dtype=jnp.float32)[None, :]
    scales = jnp.where(freq == 0, jnp.float32(1.0 / 8.0), jnp.float32((2.0 / 64.0) ** 0.5))
    return scales * jnp.cos(jnp.float32(jnp.pi) * (2.0 * place + 1.0) * freq / 128.0)


def body(momentum, activations, out_grads, positions):
    width = momentum.shape[1]
    local_cols = momentum.shape[2]
    spans = local_cols // 64
    blocks = jnp.kron(jnp.eye(spans, dtype=jnp.float32), dct_table())
    lane_ids = jnp.arange(64, dtype=jnp.int32)[None, :, None]
    gradient = lax.dot_general(
        out_grads,
        lax.all_gather(activations, "tensor", axis=0, tiled=True),
        (((0,), (0,)), ((), ())),
        preferred_element_type=jnp.float32,
    )
    accumulated = 0.9 * momentum[0].T + gradient
    coeffs = jnp.dot(blocks, accumulated, precision=lax.Precision.HIGHEST).reshape(spans, 64, width)
    picks = positions[0]
    chosen = jnp.zeros((spans, 64, width), jnp.float32)
    value_list = []
    for slot in range(4):
        hits = picks[:, slot, None, :] == lane_ids
        chosen = chosen + jnp.where(hits, 1.0, 0.0)
        value_list.append(jnp.sum(jnp.where(hits, coeffs, 0.0), axis=1))
    own_tile = coeffs * chosen
    restored = jnp.dot(
        blocks.T, own_tile.reshape(local_cols, width), precision=lax.Precision.HIGHEST
    )
    new_momentum = (accumulated - restored).T
    summed = lax.psum(own_tile.reshape(local_cols, width), "dp")
    decoded = jnp.dot(blocks.T, summed, precision=lax.Precision.HIGHEST)
    row_squares = over_copies(jnp.sum(decoded * decoded, axis=0), "tensor")
    row_scale = jnp.sqrt(row_squares / (local_cols * lax.axis_size("tensor")) + 1e-05)
    update = (decoded / row_scale[None, :]).T.astype(jnp.bfloat16)
    return (new_momentum[None], update)


def solution(mesh):
    placed = (
        P("dp", None, "tensor"),
        P(("dp", "tensor"), None),
        P("dp", "tensor"),
        P("dp", "tensor", None, None),
    )
    return jax.shard_map(
        body,
        mesh=mesh,
        in_specs=placed,
        out_specs=(P("dp", None, "tensor"), P(None, "tensor")),
        check_vma=False,
    )
```

profile of v0, /device:TPU:1, one launch (start us, length us, event | category | flops | bytes accessed | tf_op | source)
XLA Modules:
  0.0 298.3 jit_solution(9160599858302777899)
XLA Ops:
  7.2 0.0 copy-start
  7.2 0.0 all-gather.2.cloned.1.call-start
  7.2 0.7 all-gather.2.cloned.1.call-update
  7.9 0.1 mul.156
  8.0 0.1 mul.157
  8.1 0.1 cosine_multiply_fusion
  8.3 0.1 mul.169
  8.4 0.1 broadcast_multiply_fusion
  8.5 0.1 mul.177
  8.6 0.0 copy-start.3
  8.6 2.2 copy.14
  10.8 0.0 copy-done.3
  10.8 0.1 fusion.10
  11.0 116.4 %all-gather.2.cloned.1.call-done = bf16[1024,5120]{1,0:T(8,128)(2,1)} async-done(((bf16[128,5120]{1,0:T(8,128)(2,1)}), bf16[1024,5120]{1,0:T(8,128)(2,1)}) %all-gather.2.cloned.1.call-update) | async-done | bytes 10485776 | tf_op jit(solution)/shard_map/all_gather | solution.py:32
  127.4 0.0 copy-done
  127.4 5.5 %fusion.11 = f32[128,5120]{1,0:T(8,128)S(1)} fusion(bf16[1024,128]{1,0:T(8,128)(2,1)S(1)} %copy-done, bf16[1024,5120]{1,0:T(8,128)(2,1)} %all-gather.2.cloned.1.call-done), kind=kOutput, calls=%fused_computation.30 | convolution fusion | flops 1342177280 | bytes 13369344 | tf_op jit(solution)/shard_map/dot_general | solution.py:30
  133.0 0.0 copy-start.2
  133.0 5.0 %convolution_multiply_fusion = f32[2,64,5120]{2,1,0:T(8,128)} fusion(f32[128,5120]{1,0:T(8,128)S(1)} %fusion.11, f32[1,5120,128]{1,2,0:T(8,128)S(1)} %copy.14, s32[2,5120]{1,0:T(2,128)S(1)} %get-tuple-element.14, s32[2,5120]{1,0:T(2,128)S(1)} %get-tuple-element.15, s32[2,5120]{1,0:T(2,128)S(1)} %get-tuple-element.16, s32[2,5120]{1,0:T(2,128)S(1)} %get-tuple-element.17, ...), kind=kOutput, calls=%fused_computation.2 | convolution fusion | flops 1015824384 | bytes 8061952 | tf_op jit(solution)/shard_map/dot_general | solution.py:37
  138.0 0.0 copy-done.2
  138.0 6.8 %fusion = f32[1,5120,128]{1,2,0:T(8,128)} fusion(f32[128,5120]{1,0:T(8,128)} %bitcast.35, f32[128,128]{1,0:T(8,128)S(1)} %mul.177, f32[128,5120]{1,0:T(8,128)} %copy-done.2, f32[1,5120,128]{1,2,0:T(8,128)S(1)} %copy.14), kind=kOutput, calls=%fused_computation.1 | convolution fusion | flops 1008599040 | bytes 10551296 | tf_op jit(solution)/shard_map/dot_general | solution.py:46
  144.8 0.0 all-reduce.2.cloned.1.call-start
  144.9 0.7 all-reduce.2.cloned.1.call-update
  145.6 0.0 copy-start.1
  145.6 121.1 %all-reduce.2.cloned.1.call-done = f32[128,5120]{1,0:T(8,128)} async-done(((f32[128,5120]{1,0:T(8,128)}), f32[128,5120]{1,0:T(8,128)}) %all-reduce.2.cloned.1.call-update) | async-done | bytes 2621456 | tf_op jit(solution)/shard_map/psum | solution.py:50
  266.7 5.7 %multiply_reduce_fusion = (f32[5120]{0:T(1024)S(1)}, f32[128,5120]{1,0:T(8,128)}) fusion(f32[128,128]{1,0:T(8,128)S(1)} %mul.177, f32[128,5120]{1,0:T(8,128)} %all-reduce.2.cloned.1.call-done), kind=kOutput, calls=%fused_computation.7 | convolution fusion | flops 1007938560 | bytes 5328896 | tf_op jit(solution)/shard_map/dot_general | solution.py:51
  272.4 0.8 broadcast_in_dim.41
  273.1 6.7 %all-to-all-start = ((f32[8,1,5120]{2,1,0:T(1,128)}), f32[8,1,5120]{2,1,0:T(1,128)S(1)}, u32[]{:S(2)}, u32[]{:S(2)}) async-start(f32[8,1,5120]{2,1,0:T(1,128)} %broadcast_in_dim.41), calls=%async_computation | async-start | bytes 327680 | tf_op jit(solution)/shard_map/all_to_all | solution.py:9
  279.9 0.0 copy-done.1
  279.9 2.1 copy.17
  282.0 6.0 %all-to-all-done = f32[8,1,5120]{2,1,0:T(1,128)S(1)} async-done(((f32[8,1,5120]{2,1,0:T(1,128)}), f32[8,1,5120]{2,1,0:T(1,128)S(1)}, u32[]{:S(2)}, u32[]{:S(2)}) %all-to-all-start) | async-done | bytes 163872 | tf_op jit(solution)/shard_map/all_to_all | solution.py:9
  287.9 0.1 reduce_sum.19
  288.1 1.9 fusion.5
  290.0 1.4 copy.18
  (6 shorter events, 0.1 us)
Async XLA Ops:
  7.2 120.3 %copy-start = (bf16[1024,128]{1,0:T(8,128)(2,1)S(1)}, bf16[1024,128]{1,0:T(8,128)(2,1)}, u32[]{:S(2)}) copy-start(bf16[1024,128]{1,0:T(8,128)(2,1)} %param.6) | copy-start | bytes 786436
  7.2 120.3 %all-gather.2.cloned.1.call-start = ((), (), s32[]{:S(2)}) async-start(), calls=%async_computation.1 | async-start | bytes 11796480 | tf_op jit(solution)/shard_map/all_gather | solution.py:32
  8.6 2.2 copy-start.3
  133.0 5.0 %copy-start.2 = (f32[128,5120]{1,0:T(8,128)}, f32[128,5120]{1,0:T(8,128)S(1)}, u32[]{:S(2)}) copy-start(f32[128,5120]{1,0:T(8,128)S(1)} %fusion.11) | copy-start | bytes 7864324
  144.8 121.9 %all-reduce.2.cloned.1.call-start = ((), (), s32[]{:S(2)}) async-start(), calls=%async_computation.2 | async-start | bytes 5242880 | tf_op jit(solution)/shard_map/psum | solution.py:50
  145.6 134.3 %copy-start.1 = (f32[1,5120,128]{1,2,0:T(8,128)S(1)}, f32[1,5120,128]{1,2,0:T(8,128)}, u32[]{:S(2)}) copy-start(f32[1,5120,128]{1,2,0:T(8,128)} %fusion) | copy-start | bytes 7864324
  273.1 14.8 %all-to-all-start = ((f32[8,1,5120]{2,1,0:T(1,128)}), f32[8,1,5120]{2,1,0:T(1,128)S(1)}, u32[]{:S(2)}, u32[]{:S(2)}) async-start(f32[8,1,5120]{2,1,0:T(1,128)} %broadcast_in_dim.41), calls=%async_computation | async-start | bytes 327680 | tf_op jit(solution)/shard_map/all_to_all | solution.py:9
Sparse Core Ops, SparseCore 0:
  9.8 117.5 all-gather.1
  149.5 117.1 all-reduce.1
where the time goes:
time: 300 us; the launch traced here: 298 us
  waiting for transfers between devices  245 us (82%)
  matrix products  23 us (8%)
  between operations  14.1 us (5%)
  local copies, waits for them, and re-layouts  7.1 us (2%)
  starting transfers between devices  6.77 us (2%)
    psum x1, waiting for transfers between devices, body(): summed = lax.psum(own_tile.reshape(local_cols, width), 'dp')  121 us
    all_gather x1, waiting for transfers between devices, body(): lax.all_gather(activations, 'tensor', axis=0, tiled=True)  116 us
    dot_general x1, matrix products, body(): jnp.dot(blocks.T, own_tile.reshape(local_cols, width), precision=lax.Prec...  6.83 us
    all_to_all x1, starting transfers between devices, sent_to_all(): return lax.all_to_all(copies, axis, split_axis=0, concat_axis=0, tiled=True)  6.73 us
  transfers between devices with their start and end apart: 3, of which 3 were waited for; matrix products, arithmetic and copies ran while one was open for 2% of the time, Pallas kernels for 0%

commit v1 on v0

v1 whole, which is shorter than its diff:
```python
import functools

import jax
import jax.numpy as jnp
import numpy as np
from jax import lax
from jax.experimental import pallas as pl
from jax.experimental.pallas import tpu as pltpu
from jax.sharding import PartitionSpec as P

MESH = pl.DeviceIdType.MESH
HIGH = lax.Precision.HIGHEST
ROWS, COLS, TOK = 5120, 128, 128
NZ, NDP = 8, 32
CHUNK = 256
NQ = ROWS // CHUNK
TPC = CHUNK // 128
NT = ROWS // 128
SLOTS = -(-NT // NDP)

AT_FWD1, AT_FWD2, AT_SUM, AT_PASS, AT_FINISH, AT_OWN1, AT_OWN2 = 2, 4, 6, 8, 10, 11, 12


def dct_blocks():
    freq = np.arange(64, dtype=np.float64)[:, None]
    place = np.arange(64, dtype=np.float64)[None, :]
    scales = np.where(freq == 0, 1.0 / 8.0, np.sqrt(2.0 / 64.0))
    table = scales * np.cos(np.pi * (2.0 * place + 1.0) * freq / 128.0)
    return np.kron(np.eye(COLS // 64), table).astype(np.float32)


def kernel(
    a_ref, m_ref, g_ref, pos_ref, dct_ref, inv_ref,
    nm_ref, upd_ref,
    abuf, gown, gnear, gsum, mbuf, nmbuf, sout, scout, sbuf, scin,
    msg, rx, dec, sqs, ust,
    loc_sem, m_sem, nm_sem, raw_ss, raw_rs, g_ss, g_rs,
    sum_ss, sum_rs, pass_ss, msg_ss, rx_rs, sq_ss, sq_rs, up_ss, up_rs, ul_sem,
):
    me = lax.axis_index("dp")
    z = lax.axis_index("tensor")
    right = lax.rem(z + 1, NZ)
    left = lax.rem(z + NZ - 1, NZ)

    def place(q):
        return lax.rem(z + 4 - lax.rem(q, 4), 4)

    def cols(q):
        return pl.ds(pl.multiple_of(q * CHUNK, CHUNK), CHUNK)

    def owner(t):
        return lax.rem(t * 5, NDP)

    def mom_in(q):
        return pltpu.make_async_copy(m_ref.at[cols(q)], mbuf.at[q], m_sem.at[q])

    def mom_out(q):
        return pltpu.make_async_copy(nmbuf.at[q], nm_ref.at[cols(q)], nm_sem.at[q])

    def own_local(q, u):
        return pltpu.make_async_copy(a_ref.at[:, cols(q)], abuf.at[q, u], loc_sem.at[q])

    def raw(q, p, way, slot, own=False):
        return pltpu.make_async_remote_copy(
            src_ref=a_ref.at[:, cols(q)] if own else abuf.at[q, p],
            dst_ref=abuf.at[q, p],
            send_sem=raw_ss.at[q, way, slot],
            recv_sem=raw_rs.at[q, p],
            device_id={"tensor": left if way else right},
            device_id_type=MESH,
        )

    def grads(end, c, p):
        target = lax.rem(z + (NZ - 1 - c if end else 1 + c), NZ)
        block = lax.rem(target + (NZ - 3 if end else 0) + p, NZ)
        return pltpu.make_async_remote_copy(
            src_ref=g_ref.at[pl.ds(pl.multiple_of(block * TOK, TOK), TOK)],
            dst_ref=gnear.at[end, c, p],
            send_sem=g_ss.at[end, c, p],
            recv_sem=g_rs.at[end, c, p],
            device_id={"tensor": target},
            device_id_type=MESH,
        )

    def sums(q, target):
        return (
            pltpu.make_async_remote_copy(
                src_ref=sout.at[q], dst_ref=sbuf.at[q],
                send_sem=sum_ss.at[q, 0], recv_sem=sum_rs.at[q, 0],
                device_id={"tensor": target}, device_id_type=MESH,
            ),
            pltpu.make_async_remote_copy(
                src_ref=scout.at[q], dst_ref=scin.at[q],
                send_sem=sum_ss.at[q, 1], recv_sem=sum_rs.at[q, 1],
                device_id={"tensor": target}, device_id_type=MESH,
            ),
        )

    def passed(q, target):
        return (
            pltpu.make_async_remote_copy(
                src_ref=sbuf.at[q, 1], dst_ref=sbuf.at[q, 1],
                send_sem=pass_ss.at[q, 0], recv_sem=sum_rs.at[q, 0],
                device_id={"tensor": target}, device_id_type=MESH,
            ),
            pltpu.make_async_remote_copy(
                src_ref=scin.at[q], dst_ref=scin.at[q],
                send_sem=pass_ss.at[q, 1], recv_sem=sum_rs.at[q, 1],
                device_id={"tensor": target}, device_id_type=MESH,
            ),
        )

    def picks(t, source, target):
        slot = lax.div(t, NDP)
        return pltpu.make_async_remote_copy(
            src_ref=msg.at[t], dst_ref=rx.at[slot, source],
            send_sem=msg_ss.at[t], recv_sem=rx_rs.at[slot, source],
            device_id={"dp": target}, device_id_type=MESH,
        )

    def squares(slot, source, target):
        return pltpu.make_async_remote_copy(
            src_ref=sqs.at[slot, z], dst_ref=sqs.at[slot, source],
            send_sem=sq_ss.at[slot, target], recv_sem=sq_rs.at[slot, source],
            device_id={"tensor": target}, device_id_type=MESH,
        )

    def tile(t):
        return pl.ds(pl.multiple_of(t * 128, 128), 128)

    def spread(t, target):
        slot = lax.div(t, NDP)
        return pltpu.make_async_remote_copy(
            src_ref=ust.at[slot], dst_ref=upd_ref.at[tile(t)],
            send_sem=up_ss.at[slot, target], recv_sem=up_rs.at[t],
            device_id={"dp": target}, device_id_type=MESH,
        )

    def keep(t):
        slot = lax.div(t, NDP)
        return pltpu.make_async_copy(ust.at[slot], upd_ref.at[tile(t)], ul_sem.at[slot])

    def start_mom(q, _):
        mom_in(q).start()
        return 0

    lax.fori_loop(0, NQ, start_mom, 0)
    barrier = pltpu.get_barrier_semaphore()

    def greet_z(d, _):
        pl.semaphore_signal(
            barrier, inc=1, device_id={"tensor": lax.rem(z + d, NZ)}, device_id_type=MESH
        )
        return 0

    def greet_dp(d, _):
        pl.semaphore_signal(
            barrier, inc=1, device_id={"dp": lax.rem(me + d, NDP)}, device_id_type=MESH
        )
        return 0

    lax.fori_loop(1, NZ, greet_z, 0)
    lax.fori_loop(1, NDP, greet_dp, 0)
    for b in range(NZ + 3):
        block = g_ref[(b % NZ) * TOK:(b % NZ + 1) * TOK, :]
        gown[:, b * TOK:(b + 1) * TOK] = block.T
    pl.semaphore_wait(barrier, NZ + NDP - 2)

    def send_own(q):
        u = place(q)
        own_local(q, u).start()

        @pl.when(u <= 2)
        def _():
            raw(q, u, 0, 0, own=True).start()

        @pl.when(u >= 1)
        def _():
            raw(q, u, 1, 0, own=True).start()

    def send_grads():
        for c in range(2):
            for p in range(4):
                for end in range(2):
                    grads(end, c, p).start()

    def forward1(q):
        u = place(q)

        @pl.when((u == 1) | (u == 2))
        def _():
            raw(q, u - 1, 0, 1).wait_recv()
            raw(q, u - 1, 0, 1).start()
            raw(q, u + 1, 1, 1).wait_recv()
            raw(q, u + 1, 1, 1).start()

    def forward2(q):
        u = place(q)

        @pl.when(u == 2)
        def _():
            raw(q, 0, 0, 2).wait_recv()
            raw(q, 0, 0, 2).start()

        @pl.when(u == 1)
        def _():
            raw(q, 3, 1, 2).wait_recv()
            raw(q, 3, 1, 2).start()

    def make_sums(q):
        u = place(q)
        own_local(q, u).wait()

        @pl.when((u == 0) | (u == 3))
        def _():
            for p in range(4):
                @pl.when(u != p)
                def _():
                    raw(q, p, 0, 0).wait_recv()
            end = lax.div(u, 3)
            far = jnp.dot(
                gsum[end], abuf[q].reshape(4 * TOK, CHUNK), preferred_element_type=jnp.float32
            )
            for c in range(2):
                part = far[c * COLS:(c + 1) * COLS]
                top = jnp.maximum(jnp.max(jnp.abs(part), axis=0, keepdims=True), 1e-30)
                sout[q, c] = jnp.round(part * (32767.0 / top)).astype(jnp.int32).astype(jnp.int16)
                unit = top * (1.0 / 32767.0)
                for i in range(TPC):
                    scout[q, c * TPC + i:c * TPC + i + 1, :] = unit[:, i * 128:(i + 1) * 128]
            for copy in sums(q, lax.rem(z + NZ - 1 + 2 * end, NZ)):
                copy.start()

    def pass_sums(q):
        u = place(q)

        @pl.when((u == 0) | (u == 3))
        def _():
            end = lax.div(u, 3)
            for copy in sums(q, right):
                copy.wait_recv()
            for copy in passed(q, lax.rem(z + 1 + (NZ - 2) * end, NZ)):
                copy.start()

    def finish(q):
        u = place(q)
        inner = jnp.where((u == 1) | (u == 2), 1, 0)

        @pl.when(inner == 1)
        def _():
            for copy in passed(q, right):
                copy.wait_recv()

        mom_in(q).wait()
        first = lax.rem(z - u + NZ, NZ)
        near = jnp.dot(
            gown[:, pl.ds(pl.multiple_of(first * TOK, TOK), 4 * TOK)],
            abuf[q].reshape(4 * TOK, CHUNK),
            preferred_element_type=jnp.float32,
        )
        unit = jnp.concatenate(
            [scin[q, pl.ds(inner * TPC + i, 1), :] for i in range(TPC)], axis=1
        )
        accumulated = 0.9 * mbuf[q].T + (near + sbuf[q, inner].astype(jnp.float32) * unit)
        coeffs = jnp.dot(
            dct_ref[...], accumulated, precision=HIGH, preferred_element_type=jnp.float32
        )
        lanes = lax.broadcasted_iota(jnp.int32, (64, CHUNK), 0)
        kept = []
        for b in range(2):
            block = coeffs[b * 64:(b + 1) * 64]
            tile_b = jnp.zeros((64, CHUNK), jnp.float32)
            for j in range(4):
                where = pos_ref[b, j:j + 1, cols(q)]
                value = jnp.where(where == lanes, block, 0.0)
                tile_b = tile_b + value
                total = jnp.sum(value, axis=0, keepdims=True)
                spot = where.astype(jnp.float32)
                row = b * 4 + j
                for i in range(TPC):
                    part = slice(i * 128, (i + 1) * 128)
                    msg[q * TPC + i, row:row + 1, :] = total[:, part]
                    msg[q * TPC + i, row + 8:row + 9, :] = spot[:, part]
            kept.append(tile_b)

        def hand_over(i, _):
            t = q * TPC + i

            @pl.when(owner(t) == me)
            def _():
                rx[lax.div(t, NDP), me] = msg[t]

            @pl.when(owner(t) != me)
            def _():
                picks(t, me, owner(t)).start()

            return 0

        lax.fori_loop(0, TPC, hand_over, 0)
        restored = jnp.dot(
            inv_ref[...], jnp.concatenate(kept, axis=0), precision=HIGH,
            preferred_element_type=jnp.float32,
        )
        nmbuf[q] = (accumulated - restored).T
        mom_out(q).start()

    def own1(t):
        @pl.when(owner(t) == me)
        def _():
            slot = lax.div(t, NDP)

            def arrive(s, _):
                @pl.when(s != me)
                def _():
                    picks(t, s, lax.rem(me + 1, NDP)).wait_recv()
                return 0

            lax.fori_loop(0, NDP, arrive, 0)
            lanes = lax.broadcasted_iota(jnp.int32, (64, 128), 0).astype(jnp.float32)

            def add(s, totals):
                m = rx[slot, s]
                out = []
                for b in range(2):
                    total = totals[b]
                    for j in range(4):
                        row = b * 4 + j
                        total = total + jnp.where(
                            m[row + 8:row + 9] == lanes, m[row:row + 1], 0.0
                        )
                    out.append(total)
                return tuple(out)

            zero = jnp.zeros((64, 128), jnp.float32)
            totals = lax.fori_loop(0, NDP, add, (zero, zero))
            decoded = jnp.dot(
                inv_ref[...], jnp.concatenate(totals, axis=0), precision=HIGH,
                preferred_element_type=jnp.float32,
            )
            dec[slot] = decoded
            sqs[slot, z] = jnp.broadcast_to(
                jnp.sum(decoded * decoded, axis=0, keepdims=True), (8, 128)
            )

            def tell(d, _):
                squares(slot, z, lax.rem(z + d, NZ)).start()
                return 0

            lax.fori_loop(1, NZ, tell, 0)

    def own2(t):
        @pl.when(owner(t) == me)
        def _():
            slot = lax.div(t, NDP)

            def hear(d, _):
                squares(slot, lax.rem(z + d, NZ), lax.rem(z + d, NZ)).wait_recv()
                return 0

            lax.fori_loop(1, NZ, hear, 0)
            total = sqs[slot, 0, 0:1]
            for s in range(1, NZ):
                total = total + sqs[slot, s, 0:1]
            scale = jnp.sqrt(total * (1.0 / (COLS * NZ)) + 1e-05)
            ust[slot] = (dec[slot] / scale).T.astype(jnp.bfloat16)
            keep(t).start()

            def give(d, _):
                spread(t, lax.rem(me + d, NDP)).start()
                return 0

            lax.fori_loop(1, NDP, give, 0)

    def step(t, _):
        def stage(at, act):
            @pl.when((t >= at) & (t < at + NQ))
            def _():
                act(t - at)

        def tiles(act):
            def run(q):
                def one(i, _):
                    act(q * TPC + i)
                    return 0
                lax.fori_loop(0, TPC, one, 0)
            return run

        stage(AT_FWD1, forward1)
        stage(AT_FWD2, forward2)
        stage(AT_PASS, pass_sums)
        stage(0, send_own)

        @pl.when(t == 0)
        def _():
            send_grads()

        @pl.when(t == AT_SUM)
        def _():
            for end in range(2):
                for c in range(2):
                    for p in range(4):
                        grads(end, c, p).wait_recv()
                        gsum[end, c * COLS:(c + 1) * COLS, p * TOK:(p + 1) * TOK] = (
                            gnear[end, c, p].T
                        )

        stage(AT_SUM, make_sums)
        stage(AT_FINISH, finish)
        stage(AT_OWN1, tiles(own1))
        stage(AT_OWN2, tiles(own2))
        return 0

    lax.fori_loop(0, NQ + AT_OWN2, step, 0)

    for end in range(2):
        for c in range(2):
            for p in range(4):
                grads(end, c, p).wait_send()

    def drain(q, _):
        u = place(q)
        mom_out(q).wait()

        @pl.when(u <= 2)
        def _():
            raw(q, u, 0, 0, own=True).wait_send()

        @pl.when(u >= 1)
        def _():
            raw(q, u, 1, 0, own=True).wait_send()

        @pl.when((u == 1) | (u == 2))
        def _():
            raw(q, u - 1, 0, 1).wait_send()
            raw(q, u + 1, 1, 1).wait_send()

        @pl.when(u == 2)
        def _():
            raw(q, 0, 0, 2).wait_send()

        @pl.when(u == 1)
        def _():
            raw(q, 3, 1, 2).wait_send()

        @pl.when((u == 0) | (u == 3))
        def _():
            for copy in sums(q, right) + passed(q, right):
                copy.wait_send()
        return 0

    lax.fori_loop(0, NQ, drain, 0)

    def drain_tile(t, _):
        slot = lax.div(t, NDP)

        @pl.when(owner(t) == me)
        def _():
            keep(t).wait()

            def quiet(d, _):
                squares(slot, z, lax.rem(z + d, NZ)).wait_send()
                return 0

            lax.fori_loop(1, NZ, quiet, 0)

            def given(d, _):
                spread(t, lax.rem(me + d, NDP)).wait_send()
                return 0

            lax.fori_loop(1, NDP, given, 0)

        @pl.when(owner(t) != me)
        def _():
            picks(t, me, owner(t)).wait_send()
            spread(t, owner(t)).wait_recv()
        return 0

    lax.fori_loop(0, NT, drain_tile, 0)


def body(momentum, activations, out_grads, positions):
    blocks = dct_blocks()
    vmem = pl.BlockSpec(memory_space=pltpu.VMEM)
    anywhere = pl.BlockSpec(memory_space=pl.ANY)
    dma = pltpu.SemaphoreType.DMA
    new_momentum, update = pl.pallas_call(
        kernel,
        out_shape=(
            jax.ShapeDtypeStruct((ROWS, COLS), jnp.float32),
            jax.ShapeDtypeStruct((ROWS, COLS), jnp.bfloat16),
        ),
        in_specs=[anywhere, anywhere, vmem, vmem, vmem, vmem],
        out_specs=(anywhere, anywhere),
        scratch_shapes=[
            pltpu.VMEM((NQ, 4, TOK, CHUNK), jnp.bfloat16),
            pltpu.VMEM((COLS, (NZ + 3) * TOK), jnp.bfloat16),
            pltpu.VMEM((2, 2, 4, TOK, COLS), jnp.bfloat16),
            pltpu.VMEM((2, 2 * COLS, 4 * TOK), jnp.bfloat16),
            pltpu.VMEM((NQ, CHUNK, COLS), jnp.float32),
            pltpu.VMEM((NQ, CHUNK, COLS), jnp.float32),
            pltpu.VMEM((NQ, 2, COLS, CHUNK), jnp.int16),
            pltpu.VMEM((NQ, 8, 128), jnp.float32),
            pltpu.VMEM((NQ, 2, COLS, CHUNK), jnp.int16),
            pltpu.VMEM((NQ, 8, 128), jnp.float32),
            pltpu.VMEM((NT, 16, 128), jnp.float32),
            pltpu.VMEM((SLOTS, NDP, 16, 128), jnp.float32),
            pltpu.VMEM((SLOTS, COLS, 128), jnp.float32),
            pltpu.VMEM((SLOTS, NZ, 8, 128), jnp.float32),
            pltpu.VMEM((SLOTS, 128, COLS), jnp.bfloat16),
            dma((NQ,)), dma((NQ,)), dma((NQ,)),
            dma((NQ, 2, 3)), dma((NQ, 4)),
            dma((2, 2, 4)), dma((2, 2, 4)),
            dma((NQ, 2)), dma((NQ, 2)), dma((NQ, 2)),
            dma((NT,)), dma((SLOTS, NDP)),
            dma((SLOTS, NZ)), dma((SLOTS, NZ)),
            dma((SLOTS, NDP)), dma((NT,)), dma((SLOTS,)),
        ],
        compiler_params=pltpu.CompilerParams(
            collective_id=0, has_side_effects=True, vmem_limit_bytes=48 << 20
        ),
    )(activations, momentum[0], out_grads, positions[0], blocks, blocks.T)
    return new_momentum[None], update


def solution(mesh):
    placed = (
        P("dp", None, "tensor"),
        P(("dp", "tensor"), None),
        P("dp", "tensor"),
        P("dp", "tensor", None, None),
    )
    return jax.shard_map(
        body,
        mesh=mesh,
        in_specs=placed,
        out_specs=(P("dp", None, "tensor"), P(None, "tensor")),
        check_vma=False,
    )
```

time: 300 us -> 161 us (0.54)
  waiting for transfers between devices: 245 us -> 0 us
  Pallas kernels: 0 us -> 152 us
  matrix products: 23 us -> 0 us
  between operations: 14.1 us -> 0.65 us
  starting transfers between devices: 6.77 us -> 0 us
    pallas_call x0 -> x1, Pallas kernels: none -> 152 us  [body(): pl.pallas_call(kernel, out_shape=(jax.ShapeDtypeStruct((ROWS, COLS), jnp....]
    psum x1 -> x0, waiting for transfers between devices: 121 us -> none  [body(): summed = lax.psum(own_tile.reshape(local_cols, width), 'dp')]
    all_gather x1 -> x0, waiting for transfers between devices: 116 us -> none  [body(): lax.all_gather(activations, 'tensor', axis=0, tiled=True)]
    dot_general x4 -> x0, matrix products: 23 us -> none  [the longest x1 6.83 us: body(): jnp.dot(blocks.T, own_tile.reshape(local_cols, width), precision=lax.Prec...]
    all_to_all x1 -> x0, starting transfers between devices: 6.73 us -> none  [sent_to_all(): return lax.all_to_all(copies, axis, split_axis=0, concat_axis=0, tiled=True)]
    all_to_all x1 -> x0, waiting for transfers between devices: 5.97 us -> none  [sent_to_all(): return lax.all_to_all(copies, axis, split_axis=0, concat_axis=0, tiled=True)]
    unnamed x13 -> x12, local copies, waits for them, and re-layouts: 5.82 us -> 7.4 us
  transfers between devices with their start and end apart: 3 -> 0, of which waited for: 3 -> 0; matrix products, arithmetic and copies ran while one was open for 2% -> 0% of each run, Pallas kernels for 0% -> 0%
where the time goes in v1:
time: 161 us; the launch traced here: 160 us
  Pallas kernels  152 us (94%)
  local copies, waits for them, and re-layouts  7.4 us (5%)
    pallas_call x1, Pallas kernels, body(): pl.pallas_call(kernel, out_shape=(jax.ShapeDtypeStruct((ROWS, COLS), jnp....  152 us
    unnamed x12, local copies, waits for them, and re-layouts  7.4 us

profile of v1, /device:TPU:1, one launch (start us, length us, event | category | flops | bytes accessed | tf_op | source)
XLA Modules:
  0.0 160.2 jit_solution(14529028466084533663)
XLA Ops:
  0.6 0.0 copy-start
  0.6 1.3 copy-done
  1.9 0.0 copy-start.1
  2.0 0.9 copy-done.1
  2.9 0.0 copy-start.2
  2.9 0.9 copy-done.2
  3.8 0.0 copy-start.3
  3.8 0.8 copy-done.3
  4.7 0.0 copy-start.4
  4.7 0.8 copy-done.4
  5.5 152.1 %shard_map.77 = (f32[5120,128]{1,0:T(8,128)S(1)}, bf16[5120,128]{1,0:T(8,128)(2,1)S(1)}) custom-call(bf16[128,5120]{1,0:T(8,128)(2,1)S(1)} %copy-done, f32[5120,128]{1,0:T(8,128)} %bitcast.5, bf16[1024,128]{1,0:T(8,128)(2,1)S(1)} %copy-done.1, s32[2,4,5120]{2,1,0:T(4,128)S(1)} %bitcast.4, f32[128,128]{1,0:T(8,128)S(1)} %copy-done.4, f32[128,128]{1,0:T(8,128)S(1)} %copy-done.3), custom_call_target="tpu_custom_call" | custom-call | tf_op jit(solution)/shard_map/pallas_call | solution.py:486
  157.6 1.5 copy.10
  159.1 1.1 copy.11
Async XLA Ops:
  0.6 1.3 copy-start
  1.9 0.9 copy-start.1
  2.9 0.9 copy-start.2
  3.8 0.8 copy-start.3
  4.7 0.8 copy-start.4

commit v2 on v1

v2 whole, which is shorter than its diff:
```python
import functools

import jax
import jax.numpy as jnp
import numpy as np
from jax import lax
from jax.experimental import pallas as pl
from jax.experimental.pallas import tpu as pltpu
from jax.sharding import PartitionSpec as P

MESH = pl.DeviceIdType.MESH
HIGH = lax.Precision.HIGHEST
ROWS, COLS, TOK = 5120, 128, 128
NZ, NDP = 8, 32
CHUNK = 256
NQ = ROWS // CHUNK
TPC = CHUNK // 128
NT = ROWS // 128
SLOTS = -(-NT // NDP)

AT_FWD1, AT_FWD2, AT_SUM, AT_PASS, AT_FINISH = 3, 6, 9, 12, 14
AT_OWN1, AT_OWN2, AT_RELAY = 17, 22, 25


def dct_blocks():
    freq = np.arange(64, dtype=np.float64)[:, None]
    place = np.arange(64, dtype=np.float64)[None, :]
    scales = np.where(freq == 0, 1.0 / 8.0, np.sqrt(2.0 / 64.0))
    table = scales * np.cos(np.pi * (2.0 * place + 1.0) * freq / 128.0)
    return np.kron(np.eye(COLS // 64), table).astype(np.float32)


def kernel(
    a_ref, m_ref, g_ref, pos_hbm, dct_hbm,
    nm_ref, upd_ref,
    gall, pos_ref, dct_ref, inv_ref,
    abuf, gown, gnear, gsum, mbuf, nmbuf, sout, scout, sbuf, scin,
    msg, rx, dec, sqs, ust,
    loc_sem, m_sem, nm_sem, raw_ss, raw_rs, g_ss, g_rs,
    sum_ss, sum_rs, pass_ss, msg_ss, rx_rs, sq_ss, sq_rs, up_ss, up_rs, ul_sem, relay_ss, in_sem,
):
    me = lax.axis_index("dp")
    z = lax.axis_index("tensor")
    right = lax.rem(z + 1, NZ)
    left = lax.rem(z + NZ - 1, NZ)
    twin = me + 1 - 2 * lax.rem(me, 2)

    def place(q):
        return lax.rem(z + 4 - lax.rem(q, 4), 4)

    def cols(q):
        return pl.ds(pl.multiple_of(q * CHUNK, CHUNK), CHUNK)

    def owner(t):
        return lax.rem(t * 5, NDP)

    mom_in = pltpu.make_async_copy(m_ref, mbuf, m_sem)

    def mom_out(q):
        return pltpu.make_async_copy(nmbuf.at[q], nm_ref.at[cols(q)], nm_sem)

    def own_local(q):
        return pltpu.make_async_copy(a_ref.at[:, cols(q)], abuf.at[q, place(q)], loc_sem)

    def sent(ref, sem):
        pltpu.make_async_remote_copy(
            src_ref=ref, dst_ref=ref, send_sem=sem, recv_sem=sem,
            device_id={"tensor": right}, device_id_type=MESH,
        ).wait_send()

    def arrived(ref, sem):
        pltpu.make_async_remote_copy(
            src_ref=ref, dst_ref=ref, send_sem=sem, recv_sem=sem,
            device_id={"tensor": right}, device_id_type=MESH,
        ).wait_recv()

    def raw(q, p, way, own=False):
        return pltpu.make_async_remote_copy(
            src_ref=a_ref.at[:, cols(q)] if own else abuf.at[q, p],
            dst_ref=abuf.at[q, p],
            send_sem=raw_ss,
            recv_sem=raw_rs.at[q, p],
            device_id={"tensor": left if way else right},
            device_id_type=MESH,
        )

    def grads(end, c, p):
        target = lax.rem(z + (NZ - 1 - c if end else 1 + c), NZ)
        block = lax.rem(target + (NZ - 3 if end else 0) + p, NZ)
        return pltpu.make_async_remote_copy(
            src_ref=g_ref.at[pl.ds(pl.multiple_of(block * TOK, TOK), TOK)],
            dst_ref=gnear.at[end, c, p],
            send_sem=g_ss,
            recv_sem=g_rs,
            device_id={"tensor": target},
            device_id_type=MESH,
        )

    def sums(q, target):
        return (
            pltpu.make_async_remote_copy(
                src_ref=sout.at[q], dst_ref=sbuf.at[q],
                send_sem=sum_ss.at[0], recv_sem=sum_rs.at[q, 0],
                device_id={"tensor": target}, device_id_type=MESH,
            ),
            pltpu.make_async_remote_copy(
                src_ref=scout.at[q], dst_ref=scin.at[q],
                send_sem=sum_ss.at[1], recv_sem=sum_rs.at[q, 1],
                device_id={"tensor": target}, device_id_type=MESH,
            ),
        )

    def passed(q, target):
        return (
            pltpu.make_async_remote_copy(
                src_ref=sbuf.at[q, 1], dst_ref=sbuf.at[q, 1],
                send_sem=pass_ss.at[0], recv_sem=sum_rs.at[q, 0],
                device_id={"tensor": target}, device_id_type=MESH,
            ),
            pltpu.make_async_remote_copy(
                src_ref=scin.at[q], dst_ref=scin.at[q],
                send_sem=pass_ss.at[1], recv_sem=sum_rs.at[q, 1],
                device_id={"tensor": target}, device_id_type=MESH,
            ),
        )

    def picks(t, source, target):
        slot = lax.div(t, NDP)
        return pltpu.make_async_remote_copy(
            src_ref=msg.at[t], dst_ref=rx.at[slot, source],
            send_sem=msg_ss, recv_sem=rx_rs.at[slot],
            device_id={"dp": target}, device_id_type=MESH,
        )

    def squares(slot, source, target):
        return pltpu.make_async_remote_copy(
            src_ref=sqs.at[slot, z], dst_ref=sqs.at[slot, source],
            send_sem=sq_ss.at[slot], recv_sem=sq_rs.at[slot],
            device_id={"tensor": target}, device_id_type=MESH,
        )

    def tile(t):
        return pl.ds(pl.multiple_of(t * 128, 128), 128)

    def spread(t, target):
        slot = lax.div(t, NDP)
        return pltpu.make_async_remote_copy(
            src_ref=ust.at[slot], dst_ref=upd_ref.at[tile(t)],
            send_sem=up_ss.at[slot], recv_sem=up_rs.at[t],
            device_id={"dp": target}, device_id_type=MESH,
        )

    def onward(t):
        return pltpu.make_async_remote_copy(
            src_ref=upd_ref.at[tile(t)], dst_ref=upd_ref.at[tile(t)],
            send_sem=relay_ss, recv_sem=up_rs.at[t],
            device_id={"dp": twin}, device_id_type=MESH,
        )

    def keep(t):
        slot = lax.div(t, NDP)
        return pltpu.make_async_copy(ust.at[slot], upd_ref.at[tile(t)], ul_sem.at[slot])

    def start_own(q, _):
        own_local(q).start()
        return 0

    small = [
        pltpu.make_async_copy(source, target, in_sem.at[i])
        for i, (source, target) in enumerate(
            ((g_ref, gall), (pos_hbm, pos_ref), (dct_hbm, dct_ref))
        )
    ]
    for copy in small:
        copy.start()
    mom_in.start()
    lax.fori_loop(0, NQ, start_own, 0)
    barrier = pltpu.get_barrier_semaphore()

    def greet_z(d, _):
        pl.semaphore_signal(
            barrier, inc=1, device_id={"tensor": lax.rem(z + d, NZ)}, device_id_type=MESH
        )
        return 0

    def greet_dp(d, _):
        pl.semaphore_signal(
            barrier, inc=1, device_id={"dp": lax.rem(me + d, NDP)}, device_id_type=MESH
        )
        return 0

    lax.fori_loop(1, NZ, greet_z, 0)
    lax.fori_loop(1, NDP, greet_dp, 0)
    for copy in small:
        copy.wait()
    inv_ref[...] = dct_ref[...].T
    for b in range(NZ + 3):
        block = gall[(b % NZ) * TOK:(b % NZ + 1) * TOK, :]
        gown[:, b * TOK:(b + 1) * TOK] = block.T
    pl.semaphore_wait(barrier, NZ + NDP - 2)

    def send_own(q):
        u = place(q)
        @pl.when(u <= 2)
        def _():
            raw(q, u, 0, own=True).start()

        @pl.when(u >= 1)
        def _():
            raw(q, u, 1, own=True).start()

    def send_grads():
        for c in range(2):
            for p in range(4):
                for end in range(2):
                    grads(end, c, p).start()

    def forward1(q):
        u = place(q)

        @pl.when((u == 1) | (u == 2))
        def _():
            raw(q, u - 1, 0).wait_recv()
            raw(q, u - 1, 0).start()
            raw(q, u + 1, 1).wait_recv()
            raw(q, u + 1, 1).start()

    def forward2(q):
        u = place(q)

        @pl.when(u == 2)
        def _():
            raw(q, 0, 0).wait_recv()
            raw(q, 0, 0).start()

        @pl.when(u == 1)
        def _():
            raw(q, 3, 1).wait_recv()
            raw(q, 3, 1).start()

    def make_sums(q):
        u = place(q)
        @pl.when((u == 0) | (u == 3))
        def _():
            for p in range(4):
                @pl.when(u != p)
                def _():
                    raw(q, p, 0).wait_recv()
            end = lax.div(u, 3)
            far = jnp.dot(
                gsum[end], abuf[q].reshape(4 * TOK, CHUNK), preferred_element_type=jnp.float32
            )
            for c in range(2):
                part = far[c * COLS:(c + 1) * COLS]
                top = jnp.maximum(jnp.max(jnp.abs(part), axis=0, keepdims=True), 1e-30)
                sout[q, c] = jnp.round(part * (32767.0 / top)).astype(jnp.int32).astype(jnp.int16)
                unit = top * (1.0 / 32767.0)
                for i in range(TPC):
                    scout[q, c * TPC + i:c * TPC + i + 1, :] = unit[:, i * 128:(i + 1) * 128]
            for copy in sums(q, lax.rem(z + NZ - 1 + 2 * end, NZ)):
                copy.start()

    def pass_sums(q):
        u = place(q)

        @pl.when((u == 0) | (u == 3))
        def _():
            end = lax.div(u, 3)
            for copy in sums(q, right):
                copy.wait_recv()
            for copy in passed(q, lax.rem(z + 1 + (NZ - 2) * end, NZ)):
                copy.start()

    def finish(q):
        u = place(q)
        inner = jnp.where((u == 1) | (u == 2), 1, 0)

        @pl.when(inner == 1)
        def _():
            for copy in passed(q, right):
                copy.wait_recv()

        first = lax.rem(z - u + NZ, NZ)
        near = jnp.dot(
            gown[:, pl.ds(pl.multiple_of(first * TOK, TOK), 4 * TOK)],
            abuf[q].reshape(4 * TOK, CHUNK),
            preferred_element_type=jnp.float32,
        )
        unit = jnp.concatenate(
            [scin[q, pl.ds(inner * TPC + i, 1), :] for i in range(TPC)], axis=1
        )
        accumulated = 0.9 * mbuf[cols(q), :].T + (near + sbuf[q, inner].astype(jnp.float32) * unit)
        coeffs = jnp.dot(
            dct_ref[...], accumulated, precision=HIGH, preferred_element_type=jnp.float32
        )
        lanes = lax.broadcasted_iota(jnp.int32, (64, CHUNK), 0)
        kept = []
        for b in range(2):
            block = coeffs[b * 64:(b + 1) * 64]
            tile_b = jnp.zeros((64, CHUNK), jnp.float32)
            for j in range(4):
                where = pos_ref[b, j:j + 1, cols(q)]
                value = jnp.where(where == lanes, block, 0.0)
                tile_b = tile_b + value
                total = jnp.sum(value, axis=0, keepdims=True)
                spot = where.astype(jnp.float32)
                row = b * 4 + j
                for i in range(TPC):
                    part = slice(i * 128, (i + 1) * 128)
                    msg[q * TPC + i, row:row + 1, :] = total[:, part]
                    msg[q * TPC + i, row + 8:row + 9, :] = spot[:, part]
            kept.append(tile_b)

        def hand_over(i, _):
            t = q * TPC + i

            @pl.when(owner(t) == me)
            def _():
                rx[lax.div(t, NDP), me] = msg[t]

            @pl.when(owner(t) != me)
            def _():
                picks(t, me, owner(t)).start()

            return 0

        lax.fori_loop(0, TPC, hand_over, 0)
        restored = jnp.dot(
            inv_ref[...], jnp.concatenate(kept, axis=0), precision=HIGH,
            preferred_element_type=jnp.float32,
        )
        nmbuf[q] = (accumulated - restored).T
        mom_out(q).start()

    def own1(t):
        @pl.when(owner(t) == me)
        def _():
            slot = lax.div(t, NDP)

            arrived(rx.at[slot, pl.ds(0, NDP - 1)], rx_rs.at[slot])
            lanes = lax.broadcasted_iota(jnp.int32, (64, 128), 0).astype(jnp.float32)

            def add(s, totals):
                m = rx[slot, s]
                out = []
                for b in range(2):
                    total = totals[b]
                    for j in range(4):
                        row = b * 4 + j
                        total = total + jnp.where(
                            m[row + 8:row + 9] == lanes, m[row:row + 1], 0.0
                        )
                    out.append(total)
                return tuple(out)

            zero = jnp.zeros((64, 128), jnp.float32)
            summed = jnp.concatenate(
                lax.fori_loop(0, NDP, add, (zero, zero), unroll=4), axis=0
            )
            sqs[slot, z] = jnp.broadcast_to(
                jnp.sum(summed * summed, axis=0, keepdims=True), (8, 128)
            )

            def tell(d, _):
                squares(slot, z, lax.rem(z + d, NZ)).start()
                return 0

            lax.fori_loop(1, NZ, tell, 0)
            dec[slot] = jnp.dot(
                inv_ref[...], summed, precision=HIGH, preferred_element_type=jnp.float32
            )

    def own2(t):
        @pl.when(owner(t) == me)
        def _():
            slot = lax.div(t, NDP)

            arrived(sqs.at[slot, pl.ds(0, NZ - 1)], sq_rs.at[slot])
            total = sqs[slot, 0, 0:1]
            for s in range(1, NZ):
                total = total + sqs[slot, s, 0:1]
            scale = jnp.sqrt(total * (1.0 / (COLS * NZ)) + 1e-05)
            ust[slot] = (dec[slot] / scale).T.astype(jnp.bfloat16)
            keep(t).start()

            def give(d, _):
                spread(t, lax.rem(me + 2 * d, NDP)).start()
                return 0

            lax.fori_loop(1, NDP // 2, give, 0)
            spread(t, twin).start()

    def relay(t):
        @pl.when((owner(t) != me) & (lax.rem(owner(t), 2) == lax.rem(me, 2)))
        def _():
            onward(t).wait_recv()
            onward(t).start()

    def step(t, _):
        def stage(at, act):
            @pl.when((t >= at) & (t < at + NQ))
            def _():
                act(t - at)

        def tiles(act):
            def run(q):
                def one(i, _):
                    act(q * TPC + i)
                    return 0
                lax.fori_loop(0, TPC, one, 0)
            return run

        stage(AT_FWD1, forward1)
        stage(AT_FWD2, forward2)
        stage(AT_PASS, pass_sums)
        stage(0, send_own)

        @pl.when(t == 0)
        def _():
            send_grads()

        @pl.when(t == AT_SUM)
        def _():
            arrived(gnear, g_rs)
            every = abuf.at[pl.ds(0, NQ // 4)]
            pltpu.make_async_copy(every, every, loc_sem).wait()
            for end in range(2):
                for c in range(2):
                    for p in range(4):
                        gsum[end, c * COLS:(c + 1) * COLS, p * TOK:(p + 1) * TOK] = (
                            gnear[end, c, p].T
                        )

        @pl.when(t == AT_FINISH)
        def _():
            mom_in.wait()

        stage(AT_SUM, make_sums)
        stage(AT_FINISH, finish)
        stage(AT_OWN1, tiles(own1))
        stage(AT_OWN2, tiles(own2))
        stage(AT_RELAY, tiles(relay))
        return 0

    lax.fori_loop(0, NQ + AT_RELAY, step, 0)

    pltpu.make_async_copy(nm_ref, nm_ref, nm_sem).wait()
    sent(gnear, g_ss)
    sent(abuf.at[pl.ds(0, 3 * NQ // 4)], raw_ss)
    sent(sout.at[pl.ds(0, NQ // 2)], sum_ss.at[0])
    sent(scout.at[pl.ds(0, NQ // 2)], sum_ss.at[1])
    sent(sbuf.at[pl.ds(0, NQ // 4)], pass_ss.at[0])
    sent(scin.at[pl.ds(0, NQ // 2)], pass_ss.at[1])

    def drain_tile(t, mine):
        @pl.when(owner(t) == me)
        def _():
            slot = lax.div(t, NDP)
            keep(t).wait()
            sent(sqs.at[slot, pl.ds(0, NZ - 1)], sq_ss.at[slot])
            sent(upd_ref.at[pl.ds(0, NDP // 2 * 128)], up_ss.at[slot])

        @pl.when(lax.rem(owner(t), 2) != lax.rem(me, 2))
        def _():
            onward(t).wait_recv()

        return mine + jnp.where(owner(t) == me, 1, 0)

    mine = lax.fori_loop(0, NT, drain_tile, 0)
    for n in (NT // NDP, SLOTS):
        @pl.when(mine == n)
        def _():
            sent(msg.at[pl.ds(0, NT - n)], msg_ss)
            sent(upd_ref.at[pl.ds(0, (NT // 2 - n) * 128)], relay_ss)


def body(momentum, activations, out_grads, positions):
    hbm = pl.BlockSpec(memory_space=pltpu.HBM)
    dma = pltpu.SemaphoreType.DMA
    new_momentum, update = pl.pallas_call(
        kernel,
        out_shape=(
            jax.ShapeDtypeStruct((ROWS, COLS), jnp.float32),
            jax.ShapeDtypeStruct((ROWS, COLS), jnp.bfloat16),
        ),
        in_specs=[hbm] * 5,
        out_specs=(hbm, hbm),
        scratch_shapes=[
            pltpu.VMEM((NZ * TOK, COLS), jnp.bfloat16),
            pltpu.VMEM((2, 4, ROWS), jnp.int32),
            pltpu.VMEM((COLS, COLS), jnp.float32),
            pltpu.VMEM((COLS, COLS), jnp.float32),
            pltpu.VMEM((NQ, 4, TOK, CHUNK), jnp.bfloat16),
            pltpu.VMEM((COLS, (NZ + 3) * TOK), jnp.bfloat16),
            pltpu.VMEM((2, 2, 4, TOK, COLS), jnp.bfloat16),
            pltpu.VMEM((2, 2 * COLS, 4 * TOK), jnp.bfloat16),
            pltpu.VMEM((ROWS, COLS), jnp.float32),
            pltpu.VMEM((NQ, CHUNK, COLS), jnp.float32),
            pltpu.VMEM((NQ, 2, COLS, CHUNK), jnp.int16),
            pltpu.VMEM((NQ, 8, 128), jnp.float32),
            pltpu.VMEM((NQ, 2, COLS, CHUNK), jnp.int16),
            pltpu.VMEM((NQ, 8, 128), jnp.float32),
            pltpu.VMEM((NT, 16, 128), jnp.float32),
            pltpu.VMEM((SLOTS, NDP, 16, 128), jnp.float32),
            pltpu.VMEM((SLOTS, COLS, 128), jnp.float32),
            pltpu.VMEM((SLOTS, NZ, 8, 128), jnp.float32),
            pltpu.VMEM((SLOTS, 128, COLS), jnp.bfloat16),
            dma, dma, dma, dma, dma((NQ, 4)),
            dma, dma,
            dma((2,)), dma((NQ, 2)), dma((2,)),
            dma, dma((SLOTS,)),
            dma((SLOTS,)), dma((SLOTS,)),
            dma((SLOTS,)), dma((NT,)), dma((SLOTS,)), dma, dma((3,)),
        ],
        compiler_params=pltpu.CompilerParams(
            collective_id=0, has_side_effects=True, vmem_limit_bytes=60 << 20
        ),
    )(activations, momentum[0], out_grads, positions[0], dct_blocks())
    return new_momentum[None], update


def solution(mesh):
    placed = (
        P("dp", None, "tensor"),
        P(("dp", "tensor"), None),
        P("dp", "tensor"),
        P("dp", "tensor", None, None),
    )
    return jax.shard_map(
        body,
        mesh=mesh,
        in_specs=placed,
        out_specs=(P("dp", None, "tensor"), P(None, "tensor")),
        check_vma=False,
    )
```

time: 161 us -> 122 us (0.76)
  Pallas kernels: 152 us -> 116 us
  local copies, waits for them, and re-layouts: 7.4 us -> 4.56 us
    pallas_call x1, Pallas kernels: 152 us -> 116 us  [body(): pl.pallas_call(kernel, out_shape=(jax.ShapeDtypeStruct((ROWS, COLS), jnp....]
    unnamed x12 -> x4, local copies, waits for them, and re-layouts: 7.4 us -> 4.56 us
where the time goes in v2:
time: 122 us
  Pallas kernels  116 us (95%)
  local copies, waits for them, and re-layouts  4.56 us (4%)
    pallas_call x1, Pallas kernels, body(): pl.pallas_call(kernel, out_shape=(jax.ShapeDtypeStruct((ROWS, COLS), jnp....  116 us
    unnamed x4, local copies, waits for them, and re-layouts  4.56 us

profile of v2, /device:TPU:1, one launch (start us, length us, event | category | flops | bytes accessed | tf_op | source)
XLA Modules:
  0.0 121.5 jit_solution(6190793086031945179)
XLA Ops:
  0.6 116.3 %shard_map.68 = (f32[5120,128]{1,0:T(8,128)}, bf16[5120,128]{1,0:T(8,128)(2,1)}) custom-call(bf16[128,5120]{1,0:T(8,128)(2,1)} %a_ref.1, f32[5120,128]{1,0:T(8,128)} %bitcast.4, bf16[1024,128]{1,0:T(8,128)(2,1)} %g_ref.1, s32[2,4,5120]{2,1,0:T(4,128)} %bitcast.5, f32[128,128]{1,0:T(8,128)} %constant.2.clone.dct_hbm), custom_call_target="tpu_custom_call" | custom-call | tf_op jit(solution)/shard_map/pallas_call | solution.py:480
  117.0 0.0 copy-start
  117.0 3.5 %copy.9 = f32[1,5120,128]{2,1,0:T(8,128)} copy(f32[1,5120,128]{2,1,0:T(8,128)} %bitcast.3) | data formatting | bytes 5242880
  120.5 0.0 copy-done
  120.5 1.1 copy.10
Async XLA Ops:
  117.0 3.5 %copy-start = (bf16[5120,128]{1,0:T(8,128)(2,1)S(1)}, bf16[5120,128]{1,0:T(8,128)(2,1)}, u32[]{:S(2)}) copy-start(bf16[5120,128]{1,0:T(8,128)(2,1)} %get-tuple-element.9) | copy-start | bytes 3932164

commit v3 on v2

--- a/solution.py
+++ b/solution.py
@@ -9,7 +9,6 @@
 from jax.sharding import PartitionSpec as P
 
 MESH = pl.DeviceIdType.MESH
-HIGH = lax.Precision.HIGHEST
 ROWS, COLS, TOK = 5120, 128, 128
 NZ, NDP = 8, 32
 CHUNK = 256
@@ -18,8 +17,8 @@
 NT = ROWS // 128
 SLOTS = -(-NT // NDP)
 
-AT_FWD1, AT_FWD2, AT_SUM, AT_PASS, AT_FINISH = 3, 6, 9, 12, 14
-AT_OWN1, AT_OWN2, AT_RELAY = 17, 22, 25
+AT_FWD1, AT_FWD2, AT_SUM, AT_PASS, AT_FINISH = 3, 6, 8, 11, 13
+AT_OWN1, AT_OWN2, AT_RELAY = 16, 21, 27
 
 
 def dct_blocks():
@@ -27,15 +26,29 @@
     place = np.arange(64, dtype=np.float64)[None, :]
     scales = np.where(freq == 0, 1.0 / 8.0, np.sqrt(2.0 / 64.0))
     table = scales * np.cos(np.pi * (2.0 * place + 1.0) * freq / 128.0)
-    return np.kron(np.eye(COLS // 64), table).astype(np.float32)
+    blocks = np.kron(np.eye(COLS // 64), table)
+    high = blocks.astype(jnp.bfloat16)
+    low = (blocks - high.astype(np.float64)).astype(jnp.bfloat16)
+    return np.stack([
+        np.concatenate([high, high, low], axis=1),
+        np.concatenate([high.T, high.T, low.T], axis=1),
+    ])
+
+
+def product(parts, x):
+    high = x.astype(jnp.bfloat16)
+    low = (x - high.astype(jnp.float32)).astype(jnp.bfloat16)
+    return jnp.dot(
+        parts, jnp.concatenate([high, low, high], axis=0), preferred_element_type=jnp.float32
+    )
 
 
 def kernel(
     a_ref, m_ref, g_ref, pos_hbm, dct_hbm,
     nm_ref, upd_ref,
-    gall, pos_ref, dct_ref, inv_ref,
+    gall, pos_ref, dct_ref,
     abuf, gown, gnear, gsum, mbuf, nmbuf, sout, scout, sbuf, scin,
-    msg, rx, dec, sqs, ust,
+    msg, rx, dec, sqs, uall,
     loc_sem, m_sem, nm_sem, raw_ss, raw_rs, g_ss, g_rs,
     sum_ss, sum_rs, pass_ss, msg_ss, rx_rs, sq_ss, sq_rs, up_ss, up_rs, ul_sem, relay_ss, in_sem,
 ):
@@ -74,9 +87,9 @@
             device_id={"tensor": right}, device_id_type=MESH,
         ).wait_recv()
 
-    def raw(q, p, way, own=False):
+    def raw(q, p, way):
         return pltpu.make_async_remote_copy(
-            src_ref=a_ref.at[:, cols(q)] if own else abuf.at[q, p],
+            src_ref=abuf.at[q, p],
             dst_ref=abuf.at[q, p],
             send_sem=raw_ss,
             recv_sem=raw_rs.at[q, p],
@@ -145,21 +158,17 @@
     def spread(t, target):
         slot = lax.div(t, NDP)
         return pltpu.make_async_remote_copy(
-            src_ref=ust.at[slot], dst_ref=upd_ref.at[tile(t)],
+            src_ref=uall.at[tile(t)], dst_ref=uall.at[tile(t)],
             send_sem=up_ss.at[slot], recv_sem=up_rs.at[t],
             device_id={"dp": target}, device_id_type=MESH,
         )
 
     def onward(t):
         return pltpu.make_async_remote_copy(
-            src_ref=upd_ref.at[tile(t)], dst_ref=upd_ref.at[tile(t)],
+            src_ref=uall.at[tile(t)], dst_ref=uall.at[tile(t)],
             send_sem=relay_ss, recv_sem=up_rs.at[t],
             device_id={"dp": twin}, device_id_type=MESH,
         )
-
-    def keep(t):
-        slot = lax.div(t, NDP)
-        return pltpu.make_async_copy(ust.at[slot], upd_ref.at[tile(t)], ul_sem.at[slot])
 
     def start_own(q, _):
         own_local(q).start()
@@ -193,21 +202,22 @@
     lax.fori_loop(1, NDP, greet_dp, 0)
     for copy in small:
         copy.wait()
-    inv_ref[...] = dct_ref[...].T
     for b in range(NZ + 3):
         block = gall[(b % NZ) * TOK:(b % NZ + 1) * TOK, :]
         gown[:, b * TOK:(b + 1) * TOK] = block.T
+    every = abuf.at[pl.ds(0, NQ // 4)]
+    pltpu.make_async_copy(every, every, loc_sem).wait()
     pl.semaphore_wait(barrier, NZ + NDP - 2)
 
     def send_own(q):
         u = place(q)
         @pl.when(u <= 2)
         def _():
-            raw(q, u, 0, own=True).start()
+            raw(q, u, 0).start()
 
         @pl.when(u >= 1)
         def _():
-            raw(q, u, 1, own=True).start()
+            raw(q, u, 1).start()
 
     def send_grads():
         for c in range(2):
@@ -290,9 +300,7 @@
             [scin[q, pl.ds(inner * TPC + i, 1), :] for i in range(TPC)], axis=1
         )
         accumulated = 0.9 * mbuf[cols(q), :].T + (near + sbuf[q, inner].astype(jnp.float32) * unit)
-        coeffs = jnp.dot(
-            dct_ref[...], accumulated, precision=HIGH, preferred_element_type=jnp.float32
-        )
+        coeffs = product(dct_ref[0], accumulated)
         lanes = lax.broadcasted_iota(jnp.int32, (64, CHUNK), 0)
         kept = []
         for b in range(2):
@@ -325,10 +333,7 @@
             return 0
 
         lax.fori_loop(0, TPC, hand_over, 0)
-        restored = jnp.dot(
-            inv_ref[...], jnp.concatenate(kept, axis=0), precision=HIGH,
-            preferred_element_type=jnp.float32,
-        )
+        restored = product(dct_ref[1], jnp.concatenate(kept, axis=0))
         nmbuf[q] = (accumulated - restored).T
         mom_out(q).start()
 
@@ -366,9 +371,7 @@
                 return 0
 
             lax.fori_loop(1, NZ, tell, 0)
-            dec[slot] = jnp.dot(
-                inv_ref[...], summed, precision=HIGH, preferred_element_type=jnp.float32
-            )
+            dec[slot] = product(dct_ref[1], summed)
 
     def own2(t):
         @pl.when(owner(t) == me)
@@ -380,8 +383,7 @@
             for s in range(1, NZ):
                 total = total + sqs[slot, s, 0:1]
             scale = jnp.sqrt(total * (1.0 / (COLS * NZ)) + 1e-05)
-            ust[slot] = (dec[slot] / scale).T.astype(jnp.bfloat16)
-            keep(t).start()
+            uall[tile(t), :] = (dec[slot] / scale).T.astype(jnp.bfloat16)
 
             def give(d, _):
                 spread(t, lax.rem(me + 2 * d, NDP)).start()
@@ -422,8 +424,6 @@
         @pl.when(t == AT_SUM)
         def _():
             arrived(gnear, g_rs)
-            every = abuf.at[pl.ds(0, NQ // 4)]
-            pltpu.make_async_copy(every, every, loc_sem).wait()
             for end in range(2):
                 for c in range(2):
                     for p in range(4):
@@ -456,9 +456,8 @@
         @pl.when(owner(t) == me)
         def _():
             slot = lax.div(t, NDP)
-            keep(t).wait()
             sent(sqs.at[slot, pl.ds(0, NZ - 1)], sq_ss.at[slot])
-            sent(upd_ref.at[pl.ds(0, NDP // 2 * 128)], up_ss.at[slot])
+            sent(uall.at[pl.ds(0, NDP // 2 * 128)], up_ss.at[slot])
 
         @pl.when(lax.rem(owner(t), 2) != lax.rem(me, 2))
         def _():
@@ -467,11 +466,34 @@
         return mine + jnp.where(owner(t) == me, 1, 0)
 
     mine = lax.fori_loop(0, NT, drain_tile, 0)
+    whole = pltpu.make_async_copy(uall, upd_ref, ul_sem)
+    whole.start()
     for n in (NT // NDP, SLOTS):
         @pl.when(mine == n)
         def _():
             sent(msg.at[pl.ds(0, NT - n)], msg_ss)
-            sent(upd_ref.at[pl.ds(0, (NT // 2 - n) * 128)], relay_ss)
+            sent(uall.at[pl.ds(0, (NT // 2 - n) * 128)], relay_ss)
+
+    whole.wait()
+
+
+def hand_out(nm_in, upd_in, nm_out, upd_out, nm_mid, upd_mid, sem):
+    parts = [pl.ds(k * ROWS // 8, ROWS // 8) for k in range(8)]
+    triples = [(nm_in, nm_mid, nm_out), (upd_in, upd_mid, upd_out)]
+
+    def copy(i, j, way):
+        return pltpu.make_async_copy(
+            triples[i][way].at[parts[j]], triples[i][way + 1].at[parts[j]], sem.at[way, i, j]
+        )
+
+    every = [(i, j) for j in range(8) for i in range(2)]
+    for i, j in every:
+        copy(i, j, 0).start()
+    for i, j in every:
+        copy(i, j, 0).wait()
+        copy(i, j, 1).start()
+    for i, j in every:
+        copy(i, j, 1).wait()
 
 
 def body(momentum, activations, out_grads, positions):
@@ -488,8 +510,7 @@
         scratch_shapes=[
             pltpu.VMEM((NZ * TOK, COLS), jnp.bfloat16),
             pltpu.VMEM((2, 4, ROWS), jnp.int32),
-            pltpu.VMEM((COLS, COLS), jnp.float32),
-            pltpu.VMEM((COLS, COLS), jnp.float32),
+            pltpu.VMEM((2, COLS, 3 * COLS), jnp.bfloat16),
             pltpu.VMEM((NQ, 4, TOK, CHUNK), jnp.bfloat16),
             pltpu.VMEM((COLS, (NZ + 3) * TOK), jnp.bfloat16),
             pltpu.VMEM((2, 2, 4, TOK, COLS), jnp.bfloat16),
@@ -504,18 +525,30 @@
             pltpu.VMEM((SLOTS, NDP, 16, 128), jnp.float32),
             pltpu.VMEM((SLOTS, COLS, 128), jnp.float32),
             pltpu.VMEM((SLOTS, NZ, 8, 128), jnp.float32),
-            pltpu.VMEM((SLOTS, 128, COLS), jnp.bfloat16),
+            pltpu.VMEM((ROWS, COLS), jnp.bfloat16),
             dma, dma, dma, dma, dma((NQ, 4)),
             dma, dma,
             dma((2,)), dma((NQ, 2)), dma((2,)),
             dma, dma((SLOTS,)),
             dma((SLOTS,)), dma((SLOTS,)),
-            dma((SLOTS,)), dma((NT,)), dma((SLOTS,)), dma, dma((3,)),
+            dma((SLOTS,)), dma((NT,)), dma, dma, dma((3,)),
         ],
         compiler_params=pltpu.CompilerParams(
             collective_id=0, has_side_effects=True, vmem_limit_bytes=60 << 20
         ),
     )(activations, momentum[0], out_grads, positions[0], dct_blocks())
+    shapes = (
+        jax.ShapeDtypeStruct((ROWS, COLS), jnp.float32),
+        jax.ShapeDtypeStruct((ROWS, COLS), jnp.bfloat16),
+    )
+    new_momentum, update = pl.pallas_call(
+        hand_out,
+        out_shape=shapes,
+        in_specs=[hbm] * 2,
+        out_specs=(hbm, hbm),
+        scratch_shapes=[pltpu.VMEM(s.shape, s.dtype) for s in shapes] + [dma((2, 2, 8))],
+        compiler_params=pltpu.CompilerParams(vmem_limit_bytes=62 << 20),
+    )(new_momentum, update)
     return new_momentum[None], update
 
 

time: 122 us -> 119 us (0.975)
  local copies, waits for them, and re-layouts: 4.56 us -> 0 us
  Pallas kernels: 116 us -> 119 us
    unnamed x4 -> x0, local copies, waits for them, and re-layouts: 4.56 us -> none
    pallas_call x0 -> x1, Pallas kernels: none -> 3.57 us  [body(): pl.pallas_call(hand_out, out_shape=shapes, in_specs=[hbm] * 2, out_specs=...]
    pallas_call x1, Pallas kernels: 116 us -> 115 us  [body(): pl.pallas_call(kernel, out_shape=(jax.ShapeDtypeStruct((ROWS, COLS), jnp....]
where the time goes in v3:
time: 119 us
  Pallas kernels  119 us (100%)
    pallas_call x1, Pallas kernels, body(): pl.pallas_call(kernel, out_shape=(jax.ShapeDtypeStruct((ROWS, COLS), jnp....  115 us
    pallas_call x1, Pallas kernels, body(): pl.pallas_call(hand_out, out_shape=shapes, in_specs=[hbm] * 2, out_specs=...  3.57 us

profile of v3, /device:TPU:1, one launch (start us, length us, event | category | flops | bytes accessed | tf_op | source)
XLA Modules:
  0.0 119.2 jit_solution(3463488442883436252)
XLA Ops:
  0.6 115.0 %shard_map.68 = (f32[5120,128]{1,0:T(8,128)}, bf16[5120,128]{1,0:T(8,128)(2,1)}) custom-call(bf16[128,5120]{1,0:T(8,128)(2,1)} %a_ref.1, f32[5120,128]{1,0:T(8,128)} %bitcast.3, bf16[1024,128]{1,0:T(8,128)(2,1)} %g_ref.1, s32[2,4,5120]{2,1,0:T(4,128)} %bitcast.4, bf16[2,128,384]{2,1,0:T(8,128)(2,1)} %constant.2.clone.dct_hbm), custom_call_target="tpu_custom_call" | custom-call | tf_op jit(solution)/shard_map/pallas_call | solution.py:502
  115.6 3.6 %shard_map.69 = (f32[5120,128]{1,0:T(8,128)}, bf16[5120,128]{1,0:T(8,128)(2,1)}) custom-call(f32[5120,128]{1,0:T(8,128)} %get-tuple-element.6.nm_in, bf16[5120,128]{1,0:T(8,128)(2,1)} %get-tuple-element.7.upd_in), custom_call_target="tpu_custom_call" | custom-call | tf_op jit(solution)/shard_map/pallas_call | solution.py:544

commit v4 on v3

--- a/solution.py
+++ b/solution.py
@@ -17,8 +17,8 @@
 NT = ROWS // 128
 SLOTS = -(-NT // NDP)
 
-AT_FWD1, AT_FWD2, AT_SUM, AT_PASS, AT_FINISH = 3, 6, 8, 11, 13
-AT_OWN1, AT_OWN2, AT_RELAY = 16, 21, 27
+AT_FWD1, AT_FWD2, AT_SUM, AT_PASS, AT_FINISH = 3, 5, 7, 9, 11
+AT_OWN1, AT_OWN2, AT_RELAY = 14, 19, 25
 
 
 def dct_blocks():
@@ -219,11 +219,10 @@
         def _():
             raw(q, u, 1).start()
 
-    def send_grads():
+    def send_grads(p):
         for c in range(2):
-            for p in range(4):
-                for end in range(2):
-                    grads(end, c, p).start()
+            for end in range(2):
+                grads(end, c, p).start()
 
     def forward1(q):
         u = place(q)
@@ -417,9 +416,9 @@
         stage(AT_PASS, pass_sums)
         stage(0, send_own)
 
-        @pl.when(t == 0)
-        def _():
-            send_grads()
+        @pl.when(t < 4)
+        def _():
+            send_grads(t)
 
         @pl.when(t == AT_SUM)
         def _():

time: 119 us -> 118 us (level)
  no operation moved by 1% of the time
where the time goes in v4:
time: 118 us
  Pallas kernels  118 us (100%)
    pallas_call x1, Pallas kernels, body(): pl.pallas_call(kernel, out_shape=(jax.ShapeDtypeStruct((ROWS, COLS), jnp....  114 us
    pallas_call x1, Pallas kernels, body(): pl.pallas_call(hand_out, out_shape=shapes, in_specs=[hbm] * 2, out_specs=...  3.57 us

profile of v4, /device:TPU:1, one launch (start us, length us, event | category | flops | bytes accessed | tf_op | source)
XLA Modules:
  0.0 118.1 jit_solution(14334300955131077893)
XLA Ops:
  0.6 113.9 %shard_map.68 = (f32[5120,128]{1,0:T(8,128)}, bf16[5120,128]{1,0:T(8,128)(2,1)}) custom-call(bf16[128,5120]{1,0:T(8,128)(2,1)} %a_ref.1, f32[5120,128]{1,0:T(8,128)} %bitcast.3, bf16[1024,128]{1,0:T(8,128)(2,1)} %g_ref.1, s32[2,4,5120]{2,1,0:T(4,128)} %bitcast.4, bf16[2,128,384]{2,1,0:T(8,128)(2,1)} %constant.2.clone.dct_hbm), custom_call_target="tpu_custom_call" | custom-call | tf_op jit(solution)/shard_map/pallas_call | solution.py:501
  114.6 3.6 %shard_map.69 = (f32[5120,128]{1,0:T(8,128)}, bf16[5120,128]{1,0:T(8,128)(2,1)}) custom-call(f32[5120,128]{1,0:T(8,128)} %get-tuple-element.6.nm_in, bf16[5120,128]{1,0:T(8,128)(2,1)} %get-tuple-element.7.upd_in), custom_call_target="tpu_custom_call" | custom-call | tf_op jit(solution)/shard_map/pallas_call | solution.py:543

commit v5 on v4

--- a/solution.py
+++ b/solution.py
@@ -169,6 +169,9 @@
             send_sem=relay_ss, recv_sem=up_rs.at[t],
             device_id={"dp": twin}, device_id_type=MESH,
         )
+
+    def keep(t):
+        return pltpu.make_async_copy(uall.at[tile(t)], upd_ref.at[tile(t)], ul_sem)
 
     def start_own(q, _):
         own_local(q).start()
@@ -359,7 +362,7 @@
 
             zero = jnp.zeros((64, 128), jnp.float32)
             summed = jnp.concatenate(
-                lax.fori_loop(0, NDP, add, (zero, zero), unroll=4), axis=0
+                lax.fori_loop(0, NDP, add, (zero, zero), unroll=8), axis=0
             )
             sqs[slot, z] = jnp.broadcast_to(
                 jnp.sum(summed * summed, axis=0, keepdims=True), (8, 128)
@@ -462,11 +465,11 @@
         def _():
             onward(t).wait_recv()
 
+        keep(t).start()
         return mine + jnp.where(owner(t) == me, 1, 0)
 
     mine = lax.fori_loop(0, NT, drain_tile, 0)
     whole = pltpu.make_async_copy(uall, upd_ref, ul_sem)
-    whole.start()
     for n in (NT // NDP, SLOTS):
         @pl.when(mine == n)
         def _():

time: 118 us -> 118 us (level)
  no operation moved by 1% of the time
where the time goes in v5:
time: 118 us
  Pallas kernels  117 us (99%)
    pallas_call x1, Pallas kernels, body(): pl.pallas_call(kernel, out_shape=(jax.ShapeDtypeStruct((ROWS, COLS), jnp....  113 us
    pallas_call x1, Pallas kernels, body(): pl.pallas_call(hand_out, out_shape=shapes, in_specs=[hbm] * 2, out_specs=...  3.57 us

profile of v5, /device:TPU:1, one launch (start us, length us, event | category | flops | bytes accessed | tf_op | source)
XLA Modules:
  0.0 117.7 jit_solution(17645280170371284026)
XLA Ops:
  0.6 113.5 %shard_map.68 = (f32[5120,128]{1,0:T(8,128)}, bf16[5120,128]{1,0:T(8,128)(2,1)}) custom-call(bf16[128,5120]{1,0:T(8,128)(2,1)} %a_ref.1, f32[5120,128]{1,0:T(8,128)} %bitcast.3, bf16[1024,128]{1,0:T(8,128)(2,1)} %g_ref.1, s32[2,4,5120]{2,1,0:T(4,128)} %bitcast.4, bf16[2,128,384]{2,1,0:T(8,128)(2,1)} %constant.2.clone.dct_hbm), custom_call_target="tpu_custom_call" | custom-call | tf_op jit(solution)/shard_map/pallas_call | solution.py:504
  114.1 3.6 %shard_map.69 = (f32[5120,128]{1,0:T(8,128)}, bf16[5120,128]{1,0:T(8,128)(2,1)}) custom-call(f32[5120,128]{1,0:T(8,128)} %get-tuple-element.6.nm_in, bf16[5120,128]{1,0:T(8,128)(2,1)} %get-tuple-element.7.upd_in), custom_call_target="tpu_custom_call" | custom-call | tf_op jit(solution)/shard_map/pallas_call | solution.py:546
